TPU v7x, 512 devices: a whole 4x8x8 slice. The times are simulated.
512 devices in a mesh: dp: 16 (over z_lo, y), task: 32 (over z_hi, x, core).
Axes of the slice: x: 4, y: 8, z: 8 (z_hi: 4, z_lo: 2; z = z_hi * 2 + z_lo), core: 2. Of those that a mesh axis runs over, the one named last changes fastest.
Arguments:
- hidden: bfloat16 [2048, 4096], P('dp', 'task'), may hold values from -6 to 6
- proj_weight: bfloat16 [4096, 4096], P(None, 'task'), may hold values from -0.09375 to 0.09375
- task_embed: bfloat16 [8192, 512], P('task'), may hold values from -0.25 to 0.25
- event_piece: int32 [8192, 2048], P('task', 'dp'), may hold values from 0 to 7
- censored: int32 [8192, 2048], P('task', 'dp'), may hold values 0 or 1
- offset: int32 [8192, 2048], P('task', 'dp'), may hold values from 1 to 64
Outputs:
- hidden_grad: bfloat16 [4096, 2048], P('task', 'dp')
- weight_grad: bfloat16 [4096, 4096], P(None, 'task')
- embed_grad: bfloat16 [8192, 512], P('task')
All inputs are finite; a program needn't handle non-finite values. No bound on the sum of `censored` on one device may be relied on, other than what follows from the above.
Results may differ from a plain program's by a relative error of at most 0.029.
Values may be sent and summed in bfloat16 or wider, within the bound.
A program may use at most 64 MiB of HBM per device.

v0:
```python
import math

import jax
import jax.numpy as jnp
from jax import lax
from jax.sharding import PartitionSpec as P

SPAN = 64


def shards(hidden, proj_weight, task_embed, event_piece, censored, offset):
    rows = hidden.shape[0]
    cols = proj_weight.shape[1]
    rank = task_embed.shape[1]
    pieces = cols * lax.axis_size("task") // rank
    scale = 1.0 / math.sqrt(rows * lax.axis_size("dp"))
    features = lax.all_gather(hidden, "task", axis=1, tiled=True)
    proj_local = lax.dot_general(
        proj_weight, features, (((0,), (1,)), ((), ())), preferred_element_type=jnp.float32
    )
    proj_cols = proj_local.astype(jnp.bfloat16)
    proj_all = lax.all_gather(proj_cols, "task", axis=0, tiled=True)
    proj_split = proj_all.reshape(pieces, rank, rows)
    logits = jnp.einsum("tk,pkr->ptr", task_embed, proj_split, preferred_element_type=jnp.float32)
    piece_ids = lax.broadcasted_iota(jnp.int32, (pieces, 1, 1), 0)
    before = piece_ids < event_piece[None]
    inside = piece_ids == event_piece[None]
    exposure = jnp.where(
        before,
        jnp.float32(1.0),
        jnp.where(inside, offset[None].astype(jnp.float32) / SPAN, jnp.float32(0.0)),
    )
    event = (1 - censored).astype(jnp.float32)[None]
    logit_grad = ((jnp.exp(logits) * exposure - event * inside.astype(jnp.float32)) * scale).astype(
        jnp.bfloat16
    )
    embed_part = jnp.einsum(
        "ptr,pkr->tk", logit_grad, proj_split, preferred_element_type=jnp.float32
    )
    embed_sum = lax.psum(embed_part.astype(jnp.bfloat16), "dp")
    block = math.gcd(cols, rank)

    def one_block(index):
        first = index * block
        piece_index = first // rank
        within = first % rank
        embed_cols = lax.dynamic_slice_in_dim(task_embed, within, block, 1)
        grads = lax.dynamic_index_in_dim(logit_grad, piece_index, 0, keepdims=False)
        return lax.dot_general(
            embed_cols, grads, (((0,), (0,)), ((), ())), preferred_element_type=jnp.float32
        )

    blocks = lax.map(one_block, jnp.arange(cols * lax.axis_size("task") // block, dtype=jnp.int32))
    proj_grad = lax.psum_scatter(
        blocks.reshape(cols * lax.axis_size("task"), rows).astype(jnp.bfloat16),
        "task",
        scatter_dimension=0,
        tiled=True,
    )
    hidden_grad = lax.psum_scatter(
        jnp.dot(proj_weight, proj_grad, preferred_element_type=jnp.float32).astype(jnp.bfloat16),
        "task",
        scatter_dimension=0,
        tiled=True,
    )
    weight_part = lax.dot_general(
        features, proj_grad, (((0,), (1,)), ((), ())), preferred_element_type=jnp.float32
    )
    weight_out = lax.psum(weight_part.astype(jnp.bfloat16), "dp")
    return (hidden_grad, weight_out, embed_sum)


def solution(mesh):
    return jax.shard_map(
        shards,
        mesh=mesh,
        in_specs=(
            P("dp", "task"),
            P(None, "task"),
            P("task", None),
            P("task", "dp"),
            P("task", "dp"),
            P("task", "dp"),
        ),
        out_specs=(P("task", "dp"), P(None, "task"), P("task", None)),
        check_vma=False,
    )
```

profile of v0, /device:TPU:1, one launch (start us, length us, event | category | flops | bytes accessed | tf_op | source)
XLA Modules:
  0.0 551.4 jit_solution(13386781931641852580)
XLA Ops:
  8.0 67.3 %all-gather.3.cloned.1.call-done = bf16[128,4096]{1,0:T(8,128)(2,1)} async-done(((bf16[128,128]{1,0:T(8,128)(2,1)}), bf16[128,4096]{1,0:T(8,128)(2,1)}) %all-gather.3.cloned.1.call-update) | async-done | bytes 1048592 | tf_op jit(solution)/shard_map/all_gather | solution.py:17
  75.3 2.3 convolution_convert_fusion.2
  78.1 55.8 %all-gather.5.cloned.1.call-done = bf16[4096,128]{1,0:T(8,128)(2,1)} async-done(((bf16[128,128]{1,0:T(8,128)(2,1)}), bf16[4096,128]{1,0:T(8,128)(2,1)}) %all-gather.5.cloned.1.call-update) | async-done | bytes 1048592 | tf_op jit(solution)/shard_map/all_gather | solution.py:22
  133.9 1.8 fusion.11
  135.7 69.6 %while.12 = (s32[]{:T(128)}, bf16[32,128,128]{2,1,0:T(8,128)(2,1)}, s32[32]{0:T(128)S(1)}, bf16[256,512]{1,0:T(8,128)(2,1)S(1)}, bf16[8,256,128]{1,2,0:T(8,128)(...) while((s32[]{:T(128)}, bf16[32,128,128]{2,1,0:T(8,128)(2,1)}, ...), condition=%wide.region_1.2_spmd, body=%wide.region_0.1_spmd.sunk | while | flops 8388636 | bytes 197032 | solution.py:53
  139.1 0.9 fusion.28
  141.3 0.9 fusion.28
  143.5 0.9 fusion.28
  145.7 0.9 fusion.28
  147.8 0.9 fusion.28
  152.2 0.9 fusion.28
  154.4 0.9 fusion.28
  156.5 0.9 fusion.28
  158.7 0.9 fusion.28
  160.9 0.9 fusion.28
  165.2 0.9 fusion.28
  169.6 0.9 fusion.28
  173.9 0.9 fusion.28
  178.3 0.9 fusion.28
  182.6 0.9 fusion.28
  187.0 0.9 fusion.28
  191.3 0.9 fusion.28
  195.7 0.9 fusion.28
  200.0 0.9 fusion.28
  204.4 0.9 fusion.28
  205.3 2.5 fusion.12
  207.8 90.4 %reduce-scatter.5.cloned.1.call-done = bf16[128,128]{1,0:T(8,128)(2,1)} async-done(((bf16[4096,128]{1,0:T(8,128)(2,1)}), bf16[128,128]{1,0:T(8,128)(2,1)}) %reduce-scatter.5.cloned.1.call-update) | async-done | bytes 32784 | tf_op jit(solution)/shard_map/reduce_scatter | solution.py:54
  298.3 2.1 fusion.6
  301.6 1.3 copy.27
  303.0 132.0 %all-reduce.3.cloned.1.call-done = (bf16[4096,128]{0,1:T(8,128)(2,1)}, bf16[256,512]{1,0:T(8,128)(2,1)}) async-done(((bf16[4096,128]{0,1:T(8,128)(2,1)}, bf16[256,512]{1,0:T(8,128)(2,1)}), (bf16[4096,128]{0,1:T(8,128)(2,1)}, bf16[256,512]{1,0:T(8,128)(2,1)})) %all-reduce.3.cloned.1.call-update) | async-done | bytes 1310736 | tf_op jit(solution)/shard_map/psum | solution.py:69
  435.0 2.3 copy.24
  437.3 106.9 %reduce-scatter.7.cloned.1.call-done = bf16[128,128]{1,0:T(8,128)(2,1)} async-done(((bf16[4096,128]{1,0:T(8,128)(2,1)}), bf16[128,128]{1,0:T(8,128)(2,1)}) %reduce-scatter.7.cloned.1.call-update) | async-done | bytes 32784
  (79 shorter events, 32.6 us)
Async XLA Ops:
  7.2 68.1 %copy-start = (bf16[4096,128]{1,0:T(8,128)(2,1)S(1)}, bf16[4096,128]{1,0:T(8,128)(2,1)}, u32[]{:S(2)}) copy-start(bf16[4096,128]{1,0:T(8,128)(2,1)} %param.9) | copy-start | bytes 3145732
  7.2 68.1 %all-gather.3.cloned.1.call-start = ((), (), s32[]{:S(2)}) async-start(), calls=%async_computation.2 | async-start | bytes 1081344 | tf_op jit(solution)/shard_map/all_gather | solution.py:17
  7.9 69.8 %copy-start.5 = (s32[256,128]{1,0:T(8,128)S(1)}, s32[256,128]{1,0:T(8,128)}, u32[]{:S(2)}) copy-start(s32[256,128]{1,0:T(8,128)} %param.11) | copy-start | bytes 393220
  7.9 69.9 %copy-start.6 = (s32[256,128]{1,0:T(8,128)S(1)}, s32[256,128]{1,0:T(8,128)}, u32[]{:S(2)}) copy-start(s32[256,128]{1,0:T(8,128)} %param.12) | copy-start | bytes 393220
  7.9 70.0 %copy-start.7 = (s32[256,128]{1,0:T(8,128)S(1)}, s32[256,128]{1,0:T(8,128)}, u32[]{:S(2)}) copy-start(s32[256,128]{1,0:T(8,128)} %param.13) | copy-start | bytes 393220
  7.9 125.9 %all-gather.5.cloned.1.call-start = ((), (), s32[]{:S(2)}) async-start(), calls=%async_computation.3 | async-start | bytes 1081344 | tf_op jit(solution)/shard_map/all_gather | solution.py:22
  77.6 56.3 %copy-start.2 = (bf16[256,512]{1,0:T(8,128)(2,1)S(1)}, bf16[256,512]{1,0:T(8,128)(2,1)}, u32[]{:S(2)}) copy-start(bf16[256,512]{1,0:T(8,128)(2,1)} %param.10) | copy-start | bytes 786436
  77.6 220.6 %reduce-scatter.5.cloned.1.call-start = ((), (), s32[]{:S(2)}) async-start(), calls=%async_computation.4 | async-start | bytes 1081344 | tf_op jit(solution)/shard_map/reduce_scatter | solution.py:54
  205.3 93.0 %copy-start.1 = (bf16[128,4096]{1,0:T(8,128)(2,1)S(1)}, bf16[128,4096]{1,0:T(8,128)(2,1)}, u32[]{:S(2)}) copy-start(bf16[128,4096]{1,0:T(8,128)(2,1)} %all-gather.3.cloned.1.call-done) | copy-start | bytes 3145732
  205.3 229.7 %all-reduce.3.cloned.1.call-start = ((), (), s32[]{:S(2)}) async-start(), calls=%async_computation.6 | async-start | bytes 2621440 | tf_op jit(solution)/shard_map/psum | solution.py:69
  300.4 0.8 copy-start.4
  300.4 243.7 %reduce-scatter.7.cloned.1.call-start = ((), (), s32[]{:S(2)}) async-start(), calls=%async_computation.5 | async-start | bytes 1081344
  435.0 109.2 %copy-start.3 = (bf16[256,512]{1,0:T(8,128)(2,1)S(1)}, bf16[256,512]{1,0:T(8,128)(2,1)}, u32[]{:S(2)}) copy-start(bf16[256,512]{1,0:T(8,128)(2,1)} %get-tuple-element.172) | copy-start | bytes 786436
Sparse Core Ops, SparseCore 0:
  11.1 64.1 all-gather.2
  79.0 54.8 all-gather.4
  205.4 92.8 reduce-scatter.4
  302.0 132.9 all-reduce.2
  440.4 103.7 reduce-scatter.6
where the time goes:
time: 553 us; the launch traced here: 551 us
  waiting for transfers between devices  453 us (82%)
  matrix products  38.2 us (7%)
  local copies, waits for them, and re-layouts  24 us (4%)
  loops' own time  22 us (4%)
  between operations  13.9 us (3%)
    psum x1, waiting for transfers between devices, shards(): weight_out = lax.psum(weight_part.astype(jnp.bfloat16), 'dp')  132 us
    unnamed x6, waiting for transfers between devices  108 us
    reduce_scatter x1, waiting for transfers between devices, shards(): lax.psum_scatter(blocks.reshape(cols * lax.axis_size('task'), rows).astyp...  90.4 us
    all_gather x1, waiting for transfers between devices, shards(): features = lax.all_gather(hidden, 'task', axis=1, tiled=True)  67.3 us
    all_gather x1, waiting for transfers between devices, shards(): proj_all = lax.all_gather(proj_cols, 'task', axis=0, tiled=True)  55.8 us
    dot_general x32, matrix products, one_block(): lax.dot_general(embed_cols, grads, (((0,), (0,)), ((), ())), preferred_el...  28.9 us
    another operation x1, loops' own time, shards(): lax.map(one_block, jnp.arange(cols * lax.axis_size('task') // block, dtyp...  22 us
    dynamic_slice x32, local copies, waits for them, and re-layouts, shards(): lax.map(one_block, jnp.arange(cols * lax.axis_size('task') // block, dtyp...  18.6 us
  transfers between devices with their start and end apart: 5, of which 5 were waited for; matrix products, arithmetic and copies ran while one was open for 1% of the time, Pallas kernels for 0%

commit v1 on v0

v1 whole, which is shorter than its diff:
```python
import functools
import math

import jax
import jax.numpy as jnp
from jax import lax
from jax.experimental import pallas as pl
from jax.experimental.pallas import tpu as pltpu
from jax.sharding import PartitionSpec as P

SPAN = 64
B = 128
NX = 4
NZ = 4
NY = 8
MESH = pl.DeviceIdType.MESH
BF = jnp.bfloat16
F32 = jnp.float32
NSEM = 224


def dot(a, b):
    return jnp.dot(a, b, preferred_element_type=F32)


def dot_nt(a, b):
    return lax.dot_general(a, b, (((1,), (1,)), ((), ())), preferred_element_type=F32)


def kernel(
    scale,
    h_ref, w_hbm, e_hbm, ep_hbm, cen_hbm, off_hbm,
    hg_ref, wg_ref, eg_ref,
    w, e, ep, cen, off, wt, et, hbuf, pbuf, lg, fy,
    part, crecv, s1, xrecv, s2, zrecv,
    hpart, hcrecv, hs1, hxrecv, hs2, hzrecv,
    pg, pgy, wown, wpeer, epart, erecv, eown, epeer,
    lsem, ssem, rsem,
):
    dp = lax.axis_index("dp")
    t = lax.axis_index("task")
    y, zl = dp % NY, dp // NY
    core, x, zh = t % 2, (t // 2) % NX, t // (2 * NX)
    mate = 1 - core

    core_dev = (dp, t + 1 - 2 * core)
    x_dev = {i: (dp, zh * 2 * NX + ((x + i) % NX) * 2 + core) for i in range(1, NX)}
    z_dev = {i: (dp, ((zh + i) % NZ) * 2 * NX + x * 2 + core) for i in range(1, NZ)}
    y_dev = {i: (zl * NY + (y + i) % NY, t) for i in range(1, NY)}
    zl_dev = ((1 - zl) * NY + y, t)
    near_y = (1, 7, 2, 6, 3, 5, 4)
    near = (1, 3, 2)

    ids = {}
    sent = []

    def send(src, dst, key, dev):
        slot = ids.setdefault(key, len(ids))
        copy = pltpu.make_async_remote_copy(
            src, dst, ssem.at[len(sent)], rsem.at[slot], device_id=dev, device_id_type=MESH
        )
        copy.start()
        sent.append(copy)

    def arrive(dst, key):
        slot = ids.setdefault(key, len(ids))
        pltpu.make_async_remote_copy(
            dst, dst, ssem.at[0], rsem.at[slot], device_id=core_dev, device_id_type=MESH
        ).wait_recv()

    loads = [
        pltpu.make_async_copy(src, dst, lsem.at[i])
        for i, (src, dst) in enumerate(
            ((w_hbm, w), (e_hbm, e), (ep_hbm, ep), (cen_hbm, cen), (off_hbm, off))
        )
    ]
    for copy in loads:
        copy.start()

    barrier = pltpu.get_barrier_semaphore()
    peers = [core_dev, zl_dev, *x_dev.values(), *z_dev.values(), *y_dev.values()]
    for dev in peers:
        pl.semaphore_signal(barrier, inc=1, device_id=dev, device_id_type=MESH)
    hbuf[t] = jnp.transpose(h_ref[...].astype(F32)).astype(BF)
    pl.semaphore_wait(barrier, len(peers))

    def block(q, i, c):
        return ((zh + q) % NZ) * 2 * NX + ((x + i) % NX) * 2 + c

    def spread(buf, name, q):
        mine = buf.at[block(q, 0, core)]
        for i in near:
            send(mine, mine, (name, "x", (NX - i) % NX, q), x_dev[i])
        send(mine, mine, (name, "c", 0, q), core_dev)

    def gather_start(buf, name):
        mine = buf.at[t]
        for q in near:
            send(mine, mine, (name, "z", (NZ - q) % NZ), z_dev[q])
        spread(buf, name, 0)

    def gather_finish(buf, name):
        def from_z(q):
            arrive(buf.at[block(q, 0, core)], (name, "z", q))
            spread(buf, name, q)

        def from_x(q):
            for i in near:
                got = buf.at[block(q, i, core)]
                arrive(got, (name, "x", i, q))
                send(got, got, (name, "c", i, q), core_dev)

        from_z(1)
        from_z(3)
        from_x(0)
        from_z(2)
        from_x(1)
        from_x(3)
        from_x(2)
        for q in (0, 1, 3, 2):
            for i in range(NX):
                arrive(buf.at[block(q, i, mate)], (name, "c", i, q))

    gather_start(hbuf, "h")
    loads[0].wait()
    loads[1].wait()
    for i in range(32):
        wt[:, i * B:(i + 1) * B] = jnp.transpose(w[i * B:(i + 1) * B, :].astype(F32)).astype(BF)
    for i in range(4):
        et[i * B:(i + 1) * B, :] = jnp.transpose(e[:, i * B:(i + 1) * B].astype(F32)).astype(BF)
    for copy in loads[2:]:
        copy.wait()
    gather_finish(hbuf, "h")

    pbuf[t] = dot(wt[...], hbuf[...].reshape(32 * B, B)).astype(BF)
    gather_start(pbuf, "p")
    for i in near_y:
        there = (y + i) % NY
        send(hbuf.at[pl.ds(there * 4, 4)], fy.at[y], ("f", NY - i), y_dev[i])
    gather_finish(pbuf, "p")

    def core_step(p, r, name, q):
        send(p.at[q, mate], r.at[q], (name, "c", q), core_dev)

    def x_step(p, r, s, xr, name, q):
        arrive(r.at[q], (name, "c", q))
        for i in (*near, 0):
            there = (x + i) % NX
            total = p[q, core, there].astype(F32) + r[q, there].astype(F32)
            s[q, i] = total.astype(BF)
            if i:
                send(s.at[q, i], xr.at[q, NX - i], (name, "x", NX - i, q), x_dev[i])

    def z_step(s, xr, s2, zr, name, q):
        total = s[q, 0].astype(F32)
        for i in near:
            arrive(xr.at[q, i], (name, "x", i, q))
            total += xr[q, i].astype(F32)
        if q:
            s2[q] = total.astype(BF)
            send(s2.at[q], zr.at[NZ - q], (name, "z", NZ - q), z_dev[q])
        return total

    def last_step(total, zr, name):
        for q in near:
            arrive(zr.at[q], (name, "z", q))
            total += zr[q].astype(F32)
        return total

    offset = off[...].astype(F32) * (1.0 / SPAN)
    event = (1 - cen[...]).astype(F32)
    piece = ep[...]

    def grads(q):
        zq = (zh + q) % NZ
        for h in range(2):
            p = zq * 2 + h
            proj = pbuf[pl.ds(p * 4, 4)].reshape(4 * B, B)
            logits = dot(e[...], proj)
            inside = piece == p
            exposure = jnp.where(piece > p, 1.0, jnp.where(inside, offset, 0.0))
            grad = (jnp.exp(logits) * exposure - jnp.where(inside, event, 0.0)) * scale
            grad = grad.astype(BF)
            lg[p] = grad
            out = dot(et[...], grad).astype(BF)
            for j in range(4):
                part[q, j % 2, 2 * h + j // 2] = out[j * B:(j + 1) * B]
        core_step(part, crecv, "g", q)

    grads(2)
    grads(1)
    x_step(part, crecv, s1, xrecv, "g", 2)
    grads(3)
    x_step(part, crecv, s1, xrecv, "g", 1)
    grads(0)
    x_step(part, crecv, s1, xrecv, "g", 3)
    x_step(part, crecv, s1, xrecv, "g", 0)

    total = jnp.zeros(e.shape, F32)
    for p in range(8):
        total += dot_nt(lg[p], pbuf[4 * p:4 * p + 4].reshape(4 * B, B))
    epart[...] = total.astype(BF).reshape(epart.shape)
    for i in near_y:
        send(epart.at[(y + i) % NY], erecv.at[NY - i], ("e", NY - i), y_dev[i])

    for q in (2, 1, 3):
        z_step(s1, xrecv, s2, zrecv, "g", q)
    total = z_step(s1, xrecv, s2, zrecv, "g", 0)
    total = last_step(total, zrecv, "g")
    grad = total.astype(BF)
    pg[...] = jnp.transpose(total).astype(BF)
    for i in near_y:
        send(pg, pgy.at[y], ("pg", NY - i), y_dev[i])

    def hidden(q):
        zq = (zh + q) % NZ
        first = pl.multiple_of(zq * 2 * NX * B, 2 * NX * B)
        out = dot(w[pl.ds(first, 2 * NX * B), :], grad).astype(BF)
        for j in range(2 * NX):
            hpart[q, j % 2, j // 2] = out[j * B:(j + 1) * B]
        core_step(hpart, hcrecv, "d", q)

    hidden(2)
    hidden(1)
    x_step(hpart, hcrecv, hs1, hxrecv, "d", 2)
    hidden(3)
    x_step(hpart, hcrecv, hs1, hxrecv, "d", 1)
    hidden(0)
    x_step(hpart, hcrecv, hs1, hxrecv, "d", 3)
    x_step(hpart, hcrecv, hs1, hxrecv, "d", 0)

    total = epart[y].astype(F32)
    for i in near_y:
        arrive(erecv.at[i], ("e", i))
        total += erecv[i].astype(F32)
    eown[...] = total.astype(BF)
    send(eown, epeer, ("ez",), zl_dev)

    for q in (2, 1, 3):
        z_step(hs1, hxrecv, hs2, hzrecv, "d", q)
    hidden_total = z_step(hs1, hxrecv, hs2, hzrecv, "d", 0)

    fy[y] = hbuf[pl.ds(y * 4, 4)]
    pgy[y] = pg[...]
    for i in near_y:
        arrive(fy.at[(y + i) % NY], ("f", i))
        arrive(pgy.at[(y + i) % NY], ("pg", i))
    total = jnp.zeros((4 * B, B), F32)
    for i in range(0, NY, 2):
        feats = jnp.concatenate([fy[i].reshape(4 * B, B), fy[i + 1].reshape(4 * B, B)], 1)
        total += dot(feats, jnp.concatenate([pgy[i], pgy[i + 1]], 0))
    wown[...] = total.astype(BF)
    send(wown, wpeer, ("wz",), zl_dev)

    arrive(epeer, ("ez",))
    eg_ref[y] = (eown[...].astype(F32) + epeer[...].astype(F32)).astype(BF)
    for i in near_y:
        send(eg_ref.at[y], eg_ref.at[y], ("ey", NY - i), y_dev[i])

    arrive(wpeer, ("wz",))
    wg_ref[y] = (wown[...].astype(F32) + wpeer[...].astype(F32)).astype(BF)
    for i in near_y:
        send(wg_ref.at[y], wg_ref.at[y], ("wy", NY - i), y_dev[i])

    hg_ref[...] = last_step(hidden_total, hzrecv, "d").astype(BF)

    for i in near_y:
        arrive(eg_ref.at[(y + i) % NY], ("ey", i))
    for i in near_y:
        arrive(wg_ref.at[(y + i) % NY], ("wy", i))
    for copy in sent:
        copy.wait_send()
    assert len(sent) <= NSEM and len(ids) <= NSEM


def shards(hidden, proj_weight, task_embed, event_piece, censored, offset):
    rows = hidden.shape[0]
    scale = 1.0 / math.sqrt(rows * lax.axis_size("dp"))
    tasks, rank = task_embed.shape
    features, cols = proj_weight.shape
    vmem = pl.BlockSpec(memory_space=pltpu.VMEM)
    hbm = pl.BlockSpec(memory_space=pl.ANY)

    def reduce_buffers():
        return [
            pltpu.VMEM((NZ, 2, NX, B, B), BF),
            pltpu.VMEM((NZ, NX, B, B), BF),
            pltpu.VMEM((NZ, NX, B, B), BF),
            pltpu.VMEM((NZ, NX, B, B), BF),
            pltpu.VMEM((NZ, B, B), BF),
            pltpu.VMEM((NZ, B, B), BF),
        ]

    hidden_grad, weight_grad, embed_grad = pl.pallas_call(
        functools.partial(kernel, scale),
        out_shape=(
            jax.ShapeDtypeStruct((B, rows), BF),
            jax.ShapeDtypeStruct((NY, features // NY, cols), BF),
            jax.ShapeDtypeStruct((NY, tasks // NY, rank), BF),
        ),
        in_specs=[vmem] + [hbm] * 5,
        out_specs=(vmem, vmem, vmem),
        scratch_shapes=[
            pltpu.VMEM((features, cols), BF),
            pltpu.VMEM((tasks, rank), BF),
            pltpu.VMEM((tasks, rows), jnp.int32),
            pltpu.VMEM((tasks, rows), jnp.int32),
            pltpu.VMEM((tasks, rows), jnp.int32),
            pltpu.VMEM((cols, features), BF),
            pltpu.VMEM((rank, tasks), BF),
            pltpu.VMEM((32, B, B), BF),
            pltpu.VMEM((32, B, B), BF),
            pltpu.VMEM((8, tasks, rows), BF),
            pltpu.VMEM((NY, 4, B, B), BF),
            *reduce_buffers(),
            *reduce_buffers(),
            pltpu.VMEM((B, B), BF),
            pltpu.VMEM((NY, B, B), BF),
            pltpu.VMEM((4 * B, B), BF),
            pltpu.VMEM((4 * B, B), BF),
            pltpu.VMEM((NY, tasks // NY, rank), BF),
            pltpu.VMEM((NY, tasks // NY, rank), BF),
            pltpu.VMEM((tasks // NY, rank), BF),
            pltpu.VMEM((tasks // NY, rank), BF),
            pltpu.SemaphoreType.DMA((5,)),
            pltpu.SemaphoreType.DMA((NSEM,)),
            pltpu.SemaphoreType.DMA((NSEM,)),
        ],
        compiler_params=pltpu.CompilerParams(
            collective_id=0, has_side_effects=True, vmem_limit_bytes=48 * 2**20
        ),
    )(hidden, proj_weight, task_embed, event_piece, censored, offset)
    return (
        hidden_grad,
        weight_grad.reshape(features, cols),
        embed_grad.reshape(tasks, rank),
    )


def solution(mesh):
    return jax.shard_map(
        shards,
        mesh=mesh,
        in_specs=(
            P("dp", "task"),
            P(None, "task"),
            P("task", None),
            P("task", "dp"),
            P("task", "dp"),
            P("task", "dp"),
        ),
        out_specs=(P("task", "dp"), P(None, "task"), P("task", None)),
        check_vma=False,
    )
```

time: 553 us -> 109 us (0.20)
  waiting for transfers between devices: 453 us -> 0 us
  Pallas kernels: 0 us -> 98.6 us
  matrix products: 38.2 us -> 0 us
  loops' own time: 22 us -> 0 us
  local copies, waits for them, and re-layouts: 24 us -> 7.92 us
  between operations: 13.9 us -> 0.65 us
    psum x1 -> x0, waiting for transfers between devices: 132 us -> none  [shards(): weight_out = lax.psum(weight_part.astype(jnp.bfloat16), 'dp')]
    all_gather x2 -> x0, waiting for transfers between devices: 123 us -> none  [the longest x1 67.3 us: shards(): features = lax.all_gather(hidden, 'task', axis=1, tiled=True)]
    unnamed x6 -> x0, waiting for transfers between devices: 108 us -> none
    pallas_call x0 -> x1, Pallas kernels: none -> 98.6 us  [shards(): pl.pallas_call(functools.partial(kernel, scale), out_shape=(jax.ShapeDtyp...]
    reduce_scatter x1 -> x0, waiting for transfers between devices: 90.4 us -> none  [shards(): lax.psum_scatter(blocks.reshape(cols * lax.axis_size('task'), rows).astyp...]
    dot_general x37 -> x0, matrix products: 38.2 us -> none  [the longest x32 28.9 us: one_block(): lax.dot_general(embed_cols, grads, (((0,), (0,)), ((), ())), preferred_el...]
    another operation x1 -> x0, loops' own time: 22 us -> none  [shards(): lax.map(one_block, jnp.arange(cols * lax.axis_size('task') // block, dtyp...]
    dynamic_slice x32 -> x0, local copies, waits for them, and re-layouts: 18.6 us -> none  [shards(): lax.map(one_block, jnp.arange(cols * lax.axis_size('task') // block, dtyp...]
  transfers between devices with their start and end apart: 5 -> 0, of which waited for: 5 -> 0; matrix products, arithmetic and copies ran while one was open for 1% -> 0% of each run, Pallas kernels for 0% -> 0%
where the time goes in v1:
time: 109 us; the launch traced here: 107 us
  Pallas kernels  98.6 us (90%)
  local copies, waits for them, and re-layouts  7.92 us (7%)
    pallas_call x1, Pallas kernels, shards(): pl.pallas_call(functools.partial(kernel, scale), out_shape=(jax.ShapeDtyp...  98.6 us
    unnamed x15, local copies, waits for them, and re-layouts  7.92 us

profile of v1, /device:TPU:1, one launch (start us, length us, event | category | flops | bytes accessed | tf_op | source)
XLA Modules:
  0.0 107.2 jit_solution(7929040446183769254)
XLA Ops:
  0.6 0.0 copy-start
  0.6 1.2 %copy-done = bf16[4096,128]{1,0:T(8,128)(2,1)S(1)} copy-done((bf16[4096,128]{1,0:T(8,128)(2,1)S(1)}, bf16[4096,128]{1,0:T(8,128)(2,1)}, u32[]{:S(2)}) %copy-start) | copy-done | bytes 1048600
  1.9 0.0 copy-start.1
  1.9 0.9 copy-done.1
  2.8 0.0 copy-start.2
  2.8 0.9 copy-done.2
  3.7 0.0 copy-start.3
  3.7 0.9 copy-done.3
  4.6 0.0 copy-start.4
  4.6 0.9 copy-done.4
  5.5 0.0 copy-start.5
  5.5 0.8 copy-done.5
  6.3 98.6 %shard_map.85 = (bf16[128,128]{1,0:T(8,128)(2,1)S(1)}, bf16[8,512,128]{2,1,0:T(8,128)(2,1)S(1)}, bf16[8,32,512]{2,1,0:T(8,128)(2,1)S(1)}) custom-call(bf16[128,128]{1,0:T(8,128)(2,1)S(1)} %copy-done.5, bf16[4096,128]{1,0:T(8,128)(2,1)S(1)} %copy-done, bf16[256,512]{1,0:T(8,128)(2,1)S(1)} %copy-done.1, s32[256,128]{1,0:T(8,128)S(1)} %copy-done.2, ...), custom_call_target="tpu_custom_call" | custom-call | tf_op jit(solution)/shard_map/pallas_call | solution.py:294
  104.9 0.6 copy.12
  105.5 1.0 copy.13
  106.5 0.7 copy.14
Async XLA Ops:
  0.6 1.2 %copy-start = (bf16[4096,128]{1,0:T(8,128)(2,1)S(1)}, bf16[4096,128]{1,0:T(8,128)(2,1)}, u32[]{:S(2)}) copy-start(bf16[4096,128]{1,0:T(8,128)(2,1)} %w_hbm.1) | copy-start | bytes 3145732
  1.9 0.9 copy-start.1
  2.8 0.9 copy-start.2
  3.7 0.9 copy-start.3
  4.6 0.9 copy-start.4
  5.5 0.8 copy-start.5

commit v2 on v1

--- a/solution.py
+++ b/solution.py
@@ -81,32 +81,32 @@
     peers = [core_dev, zl_dev, *x_dev.values(), *z_dev.values(), *y_dev.values()]
     for dev in peers:
         pl.semaphore_signal(barrier, inc=1, device_id=dev, device_id_type=MESH)
-    hbuf[t] = jnp.transpose(h_ref[...].astype(F32)).astype(BF)
+    hbuf[zh, x, core] = jnp.transpose(h_ref[...].astype(F32)).astype(BF)
     pl.semaphore_wait(barrier, len(peers))
 
-    def block(q, i, c):
-        return ((zh + q) % NZ) * 2 * NX + ((x + i) % NX) * 2 + c
+    def block(buf, q, i, c):
+        return buf.at[(zh + q) % NZ, (x + i) % NX, c]
 
     def spread(buf, name, q):
-        mine = buf.at[block(q, 0, core)]
+        mine = block(buf, q, 0, core)
         for i in near:
             send(mine, mine, (name, "x", (NX - i) % NX, q), x_dev[i])
         send(mine, mine, (name, "c", 0, q), core_dev)
 
     def gather_start(buf, name):
-        mine = buf.at[t]
+        mine = block(buf, 0, 0, core)
         for q in near:
             send(mine, mine, (name, "z", (NZ - q) % NZ), z_dev[q])
         spread(buf, name, 0)
 
-    def gather_finish(buf, name):
+    def gather_finish(buf, name, between=lambda: None):
         def from_z(q):
-            arrive(buf.at[block(q, 0, core)], (name, "z", q))
+            arrive(block(buf, q, 0, core), (name, "z", q))
             spread(buf, name, q)
 
         def from_x(q):
             for i in near:
-                got = buf.at[block(q, i, core)]
+                got = block(buf, q, i, core)
                 arrive(got, (name, "x", i, q))
                 send(got, got, (name, "c", i, q), core_dev)
 
@@ -117,9 +117,10 @@
         from_x(1)
         from_x(3)
         from_x(2)
+        between()
         for q in (0, 1, 3, 2):
             for i in range(NX):
-                arrive(buf.at[block(q, i, mate)], (name, "c", i, q))
+                arrive(block(buf, q, i, mate), (name, "c", i, q))
 
     gather_start(hbuf, "h")
     loads[0].wait()
@@ -130,13 +131,16 @@
         et[i * B:(i + 1) * B, :] = jnp.transpose(e[:, i * B:(i + 1) * B].astype(F32)).astype(BF)
     for copy in loads[2:]:
         copy.wait()
-    gather_finish(hbuf, "h")
-
-    pbuf[t] = dot(wt[...], hbuf[...].reshape(32 * B, B)).astype(BF)
+
+    def features_to_planes():
+        for i in (4, 1, 7, 2, 6, 3, 5):
+            there = (y + i) % NZ
+            send(hbuf.at[there, :, core], fy.at[y, :, core], ("f", NY - i), y_dev[i])
+
+    gather_finish(hbuf, "h", features_to_planes)
+
+    pbuf[zh, x, core] = dot(wt[...], hbuf[...].reshape(32 * B, B)).astype(BF)
     gather_start(pbuf, "p")
-    for i in near_y:
-        there = (y + i) % NY
-        send(hbuf.at[pl.ds(there * 4, 4)], fy.at[y], ("f", NY - i), y_dev[i])
     gather_finish(pbuf, "p")
 
     def core_step(p, r, name, q):
@@ -175,7 +179,7 @@
         zq = (zh + q) % NZ
         for h in range(2):
             p = zq * 2 + h
-            proj = pbuf[pl.ds(p * 4, 4)].reshape(4 * B, B)
+            proj = pbuf[zq, 2 * h:2 * h + 2].reshape(4 * B, B)
             logits = dot(e[...], proj)
             inside = piece == p
             exposure = jnp.where(piece > p, 1.0, jnp.where(inside, offset, 0.0))
@@ -198,7 +202,7 @@
 
     total = jnp.zeros(e.shape, F32)
     for p in range(8):
-        total += dot_nt(lg[p], pbuf[4 * p:4 * p + 4].reshape(4 * B, B))
+        total += dot_nt(lg[p], pbuf[p // 2, 2 * (p % 2):2 * (p % 2) + 2].reshape(4 * B, B))
     epart[...] = total.astype(BF).reshape(epart.shape)
     for i in near_y:
         send(epart.at[(y + i) % NY], erecv.at[NY - i], ("e", NY - i), y_dev[i])
@@ -236,38 +240,49 @@
     eown[...] = total.astype(BF)
     send(eown, epeer, ("ez",), zl_dev)
 
+    chunk = y % NZ
+    for i in near_y:
+        got = fy.at[(y + i) % NY, :, core]
+        arrive(got, ("f", i))
+        send(got, got, ("fc", i), core_dev)
+    fy[y] = hbuf[chunk]
+    pgy[y] = pg[...]
+
+    arrive(epeer, ("ez",))
+    eg_ref[y] = (eown[...].astype(F32) + epeer[...].astype(F32)).astype(BF)
+    for i in near_y:
+        send(eg_ref.at[y], eg_ref.at[y], ("ey", NY - i), y_dev[i])
+
+    for i in near_y:
+        arrive(fy.at[(y + i) % NY, :, mate], ("fc", i))
+    for i in near_y:
+        arrive(pgy.at[(y + i) % NY], ("pg", i))
+    for j in range(NX):
+        total = jnp.zeros((2 * B, B), F32)
+        for i in range(0, NY, 2):
+            feats = jnp.concatenate([fy[k, j].reshape(2 * B, B) for k in (i, i + 1)], 1)
+            total += dot(feats, jnp.concatenate([pgy[i], pgy[i + 1]], 0))
+        wown[j] = total.astype(BF).reshape(2, B, B)
+        send(wown.at[j], wpeer.at[j], ("wz", j), zl_dev)
+
     for q in (2, 1, 3):
         z_step(hs1, hxrecv, hs2, hzrecv, "d", q)
     hidden_total = z_step(hs1, hxrecv, hs2, hzrecv, "d", 0)
 
-    fy[y] = hbuf[pl.ds(y * 4, 4)]
-    pgy[y] = pg[...]
-    for i in near_y:
-        arrive(fy.at[(y + i) % NY], ("f", i))
-        arrive(pgy.at[(y + i) % NY], ("pg", i))
-    total = jnp.zeros((4 * B, B), F32)
-    for i in range(0, NY, 2):
-        feats = jnp.concatenate([fy[i].reshape(4 * B, B), fy[i + 1].reshape(4 * B, B)], 1)
-        total += dot(feats, jnp.concatenate([pgy[i], pgy[i + 1]], 0))
-    wown[...] = total.astype(BF)
-    send(wown, wpeer, ("wz",), zl_dev)
-
-    arrive(epeer, ("ez",))
-    eg_ref[y] = (eown[...].astype(F32) + epeer[...].astype(F32)).astype(BF)
-    for i in near_y:
-        send(eg_ref.at[y], eg_ref.at[y], ("ey", NY - i), y_dev[i])
-
-    arrive(wpeer, ("wz",))
-    wg_ref[y] = (wown[...].astype(F32) + wpeer[...].astype(F32)).astype(BF)
-    for i in near_y:
-        send(wg_ref.at[y], wg_ref.at[y], ("wy", NY - i), y_dev[i])
+    for j in range(NX):
+        arrive(wpeer.at[j], ("wz", j))
+        mine = wg_ref.at[chunk, j]
+        wg_ref[chunk, j] = (wown[j].astype(F32) + wpeer[j].astype(F32)).astype(BF)
+        for i in (1, 7, 2 if j < 2 else 6):
+            send(mine, mine, ("wy", NY - i, j), y_dev[i])
 
     hg_ref[...] = last_step(hidden_total, hzrecv, "d").astype(BF)
 
     for i in near_y:
         arrive(eg_ref.at[(y + i) % NY], ("ey", i))
-    for i in near_y:
-        arrive(wg_ref.at[(y + i) % NY], ("wy", i))
+    for j in range(NX):
+        for i in (1, 7, 6 if j < 2 else 2):
+            arrive(wg_ref.at[(chunk + i) % NZ, j], ("wy", i, j))
     for copy in sent:
         copy.wait_send()
     assert len(sent) <= NSEM and len(ids) <= NSEM
@@ -295,7 +310,7 @@
         functools.partial(kernel, scale),
         out_shape=(
             jax.ShapeDtypeStruct((B, rows), BF),
-            jax.ShapeDtypeStruct((NY, features // NY, cols), BF),
+            jax.ShapeDtypeStruct((NZ, NX, 2, B, cols), BF),
             jax.ShapeDtypeStruct((NY, tasks // NY, rank), BF),
         ),
         in_specs=[vmem] + [hbm] * 5,
@@ -308,16 +323,16 @@
             pltpu.VMEM((tasks, rows), jnp.int32),
             pltpu.VMEM((cols, features), BF),
             pltpu.VMEM((rank, tasks), BF),
-            pltpu.VMEM((32, B, B), BF),
-            pltpu.VMEM((32, B, B), BF),
+            pltpu.VMEM((NZ, NX, 2, B, B), BF),
+            pltpu.VMEM((NZ, NX, 2, B, B), BF),
             pltpu.VMEM((8, tasks, rows), BF),
-            pltpu.VMEM((NY, 4, B, B), BF),
+            pltpu.VMEM((NY, NX, 2, B, B), BF),
             *reduce_buffers(),
             *reduce_buffers(),
             pltpu.VMEM((B, B), BF),
             pltpu.VMEM((NY, B, B), BF),
-            pltpu.VMEM((4 * B, B), BF),
-            pltpu.VMEM((4 * B, B), BF),
+            pltpu.VMEM((NX, 2, B, B), BF),
+            pltpu.VMEM((NX, 2, B, B), BF),
             pltpu.VMEM((NY, tasks // NY, rank), BF),
             pltpu.VMEM((NY, tasks // NY, rank), BF),
             pltpu.VMEM((tasks // NY, rank), BF),
@@ -327,7 +342,7 @@
             pltpu.SemaphoreType.DMA((NSEM,)),
         ],
         compiler_params=pltpu.CompilerParams(
-            collective_id=0, has_side_effects=True, vmem_limit_bytes=48 * 2**20
+            collective_id=0, has_side_effects=True, vmem_limit_bytes=62 * 2**20
         ),
     )(hidden, proj_weight, task_embed, event_piece, censored, offset)
     return (

time: 109 us -> 87.7 us (0.80)
  the two profiles are of different devices: /device:TPU:1 before, /device:TPU:2 now
where the time goes in v2:
time: 87.7 us; the launch traced here: 87.4 us
  Pallas kernels  82.4 us (94%)
  local copies, waits for them, and re-layouts  4.39 us (5%)
    pallas_call x1, Pallas kernels, shards(): pl.pallas_call(functools.partial(kernel, scale), out_shape=(jax.ShapeDtyp...  82.4 us
    unnamed x5, local copies, waits for them, and re-layouts  4.39 us

profile of v2, /device:TPU:2, one launch (start us, length us, event | category | flops | bytes accessed | tf_op | source)
XLA Modules:
  0.0 87.4 jit_solution(13131996544954065262)
XLA Ops:
  0.6 82.4 %shard_map.85 = (bf16[128,128]{1,0:T(8,128)(2,1)}, bf16[4,4,2,128,128]{4,3,2,1,0:T(8,128)(2,1)}, bf16[8,32,512]{2,1,0:T(8,128)(2,1)}) custom-call(bf16[128,128]{1,0:T(8,128)(2,1)} %h_ref.1, bf16[4096,128]{1,0:T(8,128)(2,1)} %w_hbm.1, bf16[256,512]{1,0:T(8,128)(2,1)} %e_hbm.1, s32[256,128]{1,0:T(8,128)} %ep_hbm.1, s32[256,128]{1,0:T(8,128)} %cen_hbm.1, ...), custom_call_target="tpu_custom_call" | custom-call | tf_op jit(solution)/shard_map/pallas_call | solution.py:309
  83.0 1.4 %copy.12 = bf16[128,128]{1,0:T(8,128)(2,1)} copy(bf16[128,128]{1,0:T(8,128)(2,1)} %get-tuple-element.12) | data formatting | bytes 65536
  84.4 0.0 copy-start
  84.4 2.3 %copy.13 = bf16[4096,128]{1,0:T(8,128)(2,1)} copy(bf16[4096,128]{1,0:T(8,128)(2,1)} %bitcast.2) | data formatting | bytes 2097152
  86.7 0.0 copy-done
  86.7 0.7 copy.14
Async XLA Ops:
  84.4 2.3 %copy-start = (bf16[8,32,512]{2,1,0:T(8,128)(2,1)S(1)}, bf16[8,32,512]{2,1,0:T(8,128)(2,1)}, u32[]{:S(2)}) copy-start(bf16[8,32,512]{2,1,0:T(8,128)(2,1)} %get-tuple-element.8) | copy-start | bytes 786436

commit v3 on v2

--- a/solution.py
+++ b/solution.py
@@ -30,12 +30,13 @@
 def kernel(
     scale,
     h_ref, w_hbm, e_hbm, ep_hbm, cen_hbm, off_hbm,
-    hg_ref, wg_ref, eg_ref,
+    hg_hbm, wg_hbm, eg_hbm,
     w, e, ep, cen, off, wt, et, hbuf, pbuf, lg, fy,
     part, crecv, s1, xrecv, s2, zrecv,
     hpart, hcrecv, hs1, hxrecv, hs2, hzrecv,
     pg, pgy, wown, wpeer, epart, erecv, eown, epeer,
-    lsem, ssem, rsem,
+    hg_ref, wg_ref, eg_ref,
+    lsem, osem, fsend, frecv, ssem, rsem,
 ):
     dp = lax.axis_index("dp")
     t = lax.axis_index("task")
@@ -48,11 +49,17 @@
     z_dev = {i: (dp, ((zh + i) % NZ) * 2 * NX + x * 2 + core) for i in range(1, NZ)}
     y_dev = {i: (zl * NY + (y + i) % NY, t) for i in range(1, NY)}
     zl_dev = ((1 - zl) * NY + y, t)
-    near_y = (1, 7, 2, 6, 3, 5, 4)
-    near = (1, 3, 2)
+    far_y = (4, 3, 5, 2, 6, 1, 7)
+    far = (1, 3, 2)
 
     ids = {}
     sent = []
+    stored = []
+
+    def store(src, dst):
+        copy = pltpu.make_async_copy(src, dst, osem.at[len(stored)])
+        copy.start()
+        stored.append(copy)
 
     def send(src, dst, key, dev):
         slot = ids.setdefault(key, len(ids))
@@ -89,38 +96,29 @@
 
     def spread(buf, name, q):
         mine = block(buf, q, 0, core)
-        for i in near:
+        for i in far:
             send(mine, mine, (name, "x", (NX - i) % NX, q), x_dev[i])
         send(mine, mine, (name, "c", 0, q), core_dev)
 
     def gather_start(buf, name):
         mine = block(buf, 0, 0, core)
-        for q in near:
+        for q in far:
             send(mine, mine, (name, "z", (NZ - q) % NZ), z_dev[q])
         spread(buf, name, 0)
 
-    def gather_finish(buf, name, between=lambda: None):
-        def from_z(q):
-            arrive(block(buf, q, 0, core), (name, "z", q))
-            spread(buf, name, q)
-
-        def from_x(q):
-            for i in near:
-                got = block(buf, q, i, core)
-                arrive(got, (name, "x", i, q))
-                send(got, got, (name, "c", i, q), core_dev)
-
-        from_z(1)
-        from_z(3)
-        from_x(0)
-        from_z(2)
-        from_x(1)
-        from_x(3)
-        from_x(2)
-        between()
-        for q in (0, 1, 3, 2):
-            for i in range(NX):
-                arrive(block(buf, q, i, mate), (name, "c", i, q))
+    def from_z(buf, name, q):
+        arrive(block(buf, q, 0, core), (name, "z", q))
+        spread(buf, name, q)
+
+    def from_x(buf, name, q):
+        for i in far:
+            got = block(buf, q, i, core)
+            arrive(got, (name, "x", i, q))
+            send(got, got, (name, "c", i, q), core_dev)
+
+    def from_core(buf, name, q):
+        for i in range(NX):
+            arrive(block(buf, q, i, mate), (name, "c", i, q))
 
     gather_start(hbuf, "h")
     loads[0].wait()
@@ -132,23 +130,48 @@
     for copy in loads[2:]:
         copy.wait()
 
-    def features_to_planes():
-        for i in (4, 1, 7, 2, 6, 3, 5):
-            there = (y + i) % NZ
-            send(hbuf.at[there, :, core], fy.at[y, :, core], ("f", NY - i), y_dev[i])
-
-    gather_finish(hbuf, "h", features_to_planes)
+    def to_planes(q):
+        zq = (zh + q) % NZ
+        near_by = (zq + NY - y) % NZ
+        for k, ahead in enumerate((near_by + NZ, near_by)):
+            copy = pltpu.make_async_remote_copy(
+                hbuf.at[zq, :, core],
+                fy.at[y, :, core],
+                fsend.at[q, k],
+                frecv.at[(NY - ahead) % NY],
+                device_id=(zl * NY + (y + ahead) % NY, t),
+                device_id_type=MESH,
+            )
+            if k:
+                pl.when(near_by != 0)(copy.start)
+                planes.append((near_by != 0, copy))
+            else:
+                copy.start()
+                planes.append((None, copy))
+
+    planes = []
+    from_z(hbuf, "h", 1)
+    from_z(hbuf, "h", 3)
+    from_x(hbuf, "h", 0)
+    to_planes(0)
+    from_z(hbuf, "h", 2)
+    from_x(hbuf, "h", 1)
+    to_planes(1)
+    from_x(hbuf, "h", 3)
+    to_planes(3)
+    from_x(hbuf, "h", 2)
+    to_planes(2)
+    for q in (0, 1, 3, 2):
+        from_core(hbuf, "h", q)
 
     pbuf[zh, x, core] = dot(wt[...], hbuf[...].reshape(32 * B, B)).astype(BF)
     gather_start(pbuf, "p")
-    gather_finish(pbuf, "p")
-
     def core_step(p, r, name, q):
         send(p.at[q, mate], r.at[q], (name, "c", q), core_dev)
 
     def x_step(p, r, s, xr, name, q):
         arrive(r.at[q], (name, "c", q))
-        for i in (*near, 0):
+        for i in (*far, 0):
             there = (x + i) % NX
             total = p[q, core, there].astype(F32) + r[q, there].astype(F32)
             s[q, i] = total.astype(BF)
@@ -157,7 +180,7 @@
 
     def z_step(s, xr, s2, zr, name, q):
         total = s[q, 0].astype(F32)
-        for i in near:
+        for i in far:
             arrive(xr.at[q, i], (name, "x", i, q))
             total += xr[q, i].astype(F32)
         if q:
@@ -166,7 +189,7 @@
         return total
 
     def last_step(total, zr, name):
-        for q in near:
+        for q in far:
             arrive(zr.at[q], (name, "z", q))
             total += zr[q].astype(F32)
         return total
@@ -191,29 +214,43 @@
                 part[q, j % 2, 2 * h + j // 2] = out[j * B:(j + 1) * B]
         core_step(part, crecv, "g", q)
 
+    def reduce_x(q):
+        x_step(part, crecv, s1, xrecv, "g", q)
+
+    from_z(pbuf, "p", 1)
+    from_z(pbuf, "p", 3)
+    from_x(pbuf, "p", 0)
+    from_z(pbuf, "p", 2)
+    from_core(pbuf, "p", 0)
+    grads(0)
+    from_x(pbuf, "p", 1)
+    from_x(pbuf, "p", 3)
+    reduce_x(0)
+    from_core(pbuf, "p", 1)
+    grads(1)
+    from_x(pbuf, "p", 2)
+    from_core(pbuf, "p", 3)
+    grads(3)
+    reduce_x(1)
+    from_core(pbuf, "p", 2)
     grads(2)
-    grads(1)
-    x_step(part, crecv, s1, xrecv, "g", 2)
-    grads(3)
-    x_step(part, crecv, s1, xrecv, "g", 1)
-    grads(0)
-    x_step(part, crecv, s1, xrecv, "g", 3)
-    x_step(part, crecv, s1, xrecv, "g", 0)
+    reduce_x(3)
+    reduce_x(2)
 
     total = jnp.zeros(e.shape, F32)
     for p in range(8):
         total += dot_nt(lg[p], pbuf[p // 2, 2 * (p % 2):2 * (p % 2) + 2].reshape(4 * B, B))
     epart[...] = total.astype(BF).reshape(epart.shape)
-    for i in near_y:
+    for i in far_y:
         send(epart.at[(y + i) % NY], erecv.at[NY - i], ("e", NY - i), y_dev[i])
 
-    for q in (2, 1, 3):
+    for q in (1, 3, 2):
         z_step(s1, xrecv, s2, zrecv, "g", q)
     total = z_step(s1, xrecv, s2, zrecv, "g", 0)
     total = last_step(total, zrecv, "g")
     grad = total.astype(BF)
     pg[...] = jnp.transpose(total).astype(BF)
-    for i in near_y:
+    for i in far_y:
         send(pg, pgy.at[y], ("pg", NY - i), y_dev[i])
 
     def hidden(q):
@@ -234,28 +271,33 @@
     x_step(hpart, hcrecv, hs1, hxrecv, "d", 0)
 
     total = epart[y].astype(F32)
-    for i in near_y:
+    for i in far_y:
         arrive(erecv.at[i], ("e", i))
         total += erecv[i].astype(F32)
     eown[...] = total.astype(BF)
     send(eown, epeer, ("ez",), zl_dev)
 
     chunk = y % NZ
-    for i in near_y:
+    for i in far_y:
         got = fy.at[(y + i) % NY, :, core]
-        arrive(got, ("f", i))
+        pltpu.make_async_remote_copy(
+            got, got, fsend.at[0, 0], frecv.at[i], device_id=core_dev, device_id_type=MESH
+        ).wait_recv()
         send(got, got, ("fc", i), core_dev)
     fy[y] = hbuf[chunk]
     pgy[y] = pg[...]
 
     arrive(epeer, ("ez",))
     eg_ref[y] = (eown[...].astype(F32) + epeer[...].astype(F32)).astype(BF)
-    for i in near_y:
+    for i in far_y:
         send(eg_ref.at[y], eg_ref.at[y], ("ey", NY - i), y_dev[i])
 
-    for i in near_y:
+    def half(ref, j, c):
+        return ref.at[j, c] if j < 2 else ref.at[j]
+
+    for i in far_y:
         arrive(fy.at[(y + i) % NY, :, mate], ("fc", i))
-    for i in near_y:
+    for i in far_y:
         arrive(pgy.at[(y + i) % NY], ("pg", i))
     for j in range(NX):
         total = jnp.zeros((2 * B, B), F32)
@@ -263,29 +305,84 @@
             feats = jnp.concatenate([fy[k, j].reshape(2 * B, B) for k in (i, i + 1)], 1)
             total += dot(feats, jnp.concatenate([pgy[i], pgy[i + 1]], 0))
         wown[j] = total.astype(BF).reshape(2, B, B)
-        send(wown.at[j], wpeer.at[j], ("wz", j), zl_dev)
-
-    for q in (2, 1, 3):
+        send(half(wown, j, 1 - zl), half(wpeer, j, 1 - zl), ("wz", j), zl_dev)
+
+    for q in (1, 3, 2):
         z_step(hs1, hxrecv, hs2, hzrecv, "d", q)
     hidden_total = z_step(hs1, hxrecv, hs2, hzrecv, "d", 0)
 
+    def pass_on(i, j):
+        got = half(wg_ref.at[(chunk + i) % NZ], j, zl)
+        send(got, got, ("wf", i, j), zl_dev)
+
     for j in range(NX):
-        arrive(wpeer.at[j], ("wz", j))
-        mine = wg_ref.at[chunk, j]
-        wg_ref[chunk, j] = (wown[j].astype(F32) + wpeer[j].astype(F32)).astype(BF)
-        for i in (1, 7, 2 if j < 2 else 6):
+        arrive(half(wpeer, j, zl), ("wz", j))
+        mine = half(wg_ref.at[chunk], j, zl)
+        mine[...] = (half(wown, j, zl)[...].astype(F32) + half(wpeer, j, zl)[...].astype(F32)).astype(BF)
+        for i in (6 if j % 2 else 2, 1, 7):
             send(mine, mine, ("wy", NY - i, j), y_dev[i])
+        if j < 2:
+            pass_on(0, j)
+        store(mine, half(wg_hbm.at[chunk], j, zl))
 
     hg_ref[...] = last_step(hidden_total, hzrecv, "d").astype(BF)
-
-    for i in near_y:
+    store(hg_ref, hg_hbm)
+
+    for i in far_y:
         arrive(eg_ref.at[(y + i) % NY], ("ey", i))
+    store(eg_ref, eg_hbm)
     for j in range(NX):
-        for i in (1, 7, 6 if j < 2 else 2):
-            arrive(wg_ref.at[(chunk + i) % NZ, j], ("wy", i, j))
+        for i in (1, 7, 2 if j % 2 else 6):
+            there = (chunk + i) % NZ
+            arrive(half(wg_ref.at[there], j, zl), ("wy", i, j))
+            if j < 2:
+                pass_on(i, j)
+            store(half(wg_ref.at[there], j, zl), half(wg_hbm.at[there], j, zl))
+    for j in range(2):
+        for i in (0, 1, 7, 2 if j % 2 else 6):
+            there = (chunk + i) % NZ
+            arrive(wg_ref.at[there, j, 1 - zl], ("wf", i, j))
+            store(wg_ref.at[there, j, 1 - zl], wg_hbm.at[there, j, 1 - zl])
+    for copy in stored:
+        copy.wait()
     for copy in sent:
         copy.wait_send()
+    for there, copy in planes:
+        if there is None:
+            copy.wait_send()
+        else:
+            pl.when(there)(copy.wait_send)
     assert len(sent) <= NSEM and len(ids) <= NSEM
+
+
+def move_kernel(hg, wg, eg, hg_out, wg_out, eg_out, hg_v, wg_v, eg_v, isem, osem):
+    moves = [(wg.at[i], wg_v.at[i], wg_out.at[i]) for i in range(NZ)]
+    moves += [(eg, eg_v, eg_out), (hg, hg_v, hg_out)]
+    loads = [pltpu.make_async_copy(a, b, isem.at[i]) for i, (a, b, _) in enumerate(moves)]
+    stores = [pltpu.make_async_copy(b, c, osem.at[i]) for i, (_, b, c) in enumerate(moves)]
+    for copy in loads:
+        copy.start()
+    for load, save in zip(loads, stores):
+        load.wait()
+        save.start()
+    for copy in stores:
+        copy.wait()
+
+
+def move_results(*results):
+    anywhere = [pl.BlockSpec(memory_space=pl.ANY)] * 3
+    return pl.pallas_call(
+        move_kernel,
+        out_shape=[jax.ShapeDtypeStruct(r.shape, r.dtype) for r in results],
+        in_specs=anywhere,
+        out_specs=anywhere,
+        scratch_shapes=[
+            *[pltpu.VMEM(r.shape, r.dtype) for r in results],
+            pltpu.SemaphoreType.DMA((NZ + 2,)),
+            pltpu.SemaphoreType.DMA((NZ + 2,)),
+        ],
+        compiler_params=pltpu.CompilerParams(vmem_limit_bytes=62 * 2**20),
+    )(*results)
 
 
 def shards(hidden, proj_weight, task_embed, event_piece, censored, offset):
@@ -314,7 +411,7 @@
             jax.ShapeDtypeStruct((NY, tasks // NY, rank), BF),
         ),
         in_specs=[vmem] + [hbm] * 5,
-        out_specs=(vmem, vmem, vmem),
+        out_specs=(hbm, hbm, hbm),
         scratch_shapes=[
             pltpu.VMEM((features, cols), BF),
             pltpu.VMEM((tasks, rank), BF),
@@ -337,7 +434,13 @@
             pltpu.VMEM((NY, tasks // NY, rank), BF),
             pltpu.VMEM((tasks // NY, rank), BF),
             pltpu.VMEM((tasks // NY, rank), BF),
+            pltpu.VMEM((B, rows), BF),
+            pltpu.VMEM((NZ, NX, 2, B, cols), BF),
+            pltpu.VMEM((NY, tasks // NY, rank), BF),
             pltpu.SemaphoreType.DMA((5,)),
+            pltpu.SemaphoreType.DMA((32,)),
+            pltpu.SemaphoreType.DMA((NZ, 2)),
+            pltpu.SemaphoreType.DMA((NY,)),
             pltpu.SemaphoreType.DMA((NSEM,)),
             pltpu.SemaphoreType.DMA((NSEM,)),
         ],
@@ -345,6 +448,7 @@
             collective_id=0, has_side_effects=True, vmem_limit_bytes=62 * 2**20
         ),
     )(hidden, proj_weight, task_embed, event_piece, censored, offset)
+    hidden_grad, weight_grad, embed_grad = move_results(hidden_grad, weight_grad, embed_grad)
     return (
         hidden_grad,
         weight_grad.reshape(features, cols),

time: 87.7 us -> 81.8 us (0.933)
  the two profiles are of different devices: /device:TPU:2 before, /device:TPU:1 now
where the time goes in v3:
time: 81.8 us; the launch traced here: 81.6 us
  Pallas kernels  80.9 us (99%)
    pallas_call x1, Pallas kernels, shards(): pl.pallas_call(functools.partial(kernel, scale), out_shape=(jax.ShapeDtyp...  78.8 us
    pallas_call x1, Pallas kernels, move_results(): pl.pallas_call(move_kernel, out_shape=[jax.ShapeDtypeStruct(r.shape, r.dt...  2.1 us

profile of v3, /device:TPU:1, one launch (start us, length us, event | category | flops | bytes accessed | tf_op | source)
XLA Modules:
  0.0 81.6 jit_solution(1691051458393833405)
XLA Ops:
  0.6 78.8 %shard_map.85 = (bf16[128,128]{1,0:T(8,128)(2,1)}, bf16[4,4,2,128,128]{4,3,2,1,0:T(8,128)(2,1)}, bf16[8,32,512]{2,1,0:T(8,128)(2,1)}) custom-call(bf16[128,128]{1,0:T(8,128)(2,1)} %h_ref.1, bf16[4096,128]{1,0:T(8,128)(2,1)} %w_hbm.1, bf16[256,512]{1,0:T(8,128)(2,1)} %e_hbm.1, s32[256,128]{1,0:T(8,128)} %ep_hbm.1, s32[256,128]{1,0:T(8,128)} %cen_hbm.1, ...), custom_call_target="tpu_custom_call" | custom-call | tf_op jit(solution)/shard_map/pallas_call | solution.py:406
  79.5 2.1 %shard_map.86 = (bf16[128,128]{1,0:T(8,128)(2,1)}, bf16[4,4,2,128,128]{4,3,2,1,0:T(8,128)(2,1)}, bf16[8,32,512]{2,1,0:T(8,128)(2,1)}) custom-call(bf16[128,128]{1,0:T(8,128)(2,1)} %get-tuple-element.9.hg, bf16[4,4,2,128,128]{4,3,2,1,0:T(8,128)(2,1)} %get-tuple-element.10.wg, bf16[8,32,512]{2,1,0:T(8,128)(2,1)} %get-tuple-element.11.eg), custom_call_target="tpu_custom_call" | custom-call | tf_op jit(solution)/shard_map/pallas_call | solution.py:374

commit v4 on v3

--- a/solution.py
+++ b/solution.py
@@ -29,9 +29,9 @@
 
 def kernel(
     scale,
-    h_ref, w_hbm, e_hbm, ep_hbm, cen_hbm, off_hbm,
+    h_hbm, w_hbm, e_hbm, ep_hbm, cen_hbm, off_hbm,
     hg_hbm, wg_hbm, eg_hbm,
-    w, e, ep, cen, off, wt, et, hbuf, pbuf, lg, fy,
+    w, e, ep, cen, off, et, hbuf, pbuf, lg, fy, ht,
     part, crecv, s1, xrecv, s2, zrecv,
     hpart, hcrecv, hs1, hxrecv, hs2, hzrecv,
     pg, pgy, wown, wpeer, epart, erecv, eown, epeer,
@@ -75,36 +75,36 @@
             dst, dst, ssem.at[0], rsem.at[slot], device_id=core_dev, device_id_type=MESH
         ).wait_recv()
 
+    barrier = pltpu.get_barrier_semaphore()
+    peers = [core_dev, zl_dev, *x_dev.values(), *z_dev.values(), *y_dev.values()]
+    for dev in peers:
+        pl.semaphore_signal(barrier, inc=1, device_id=dev, device_id_type=MESH)
     loads = [
         pltpu.make_async_copy(src, dst, lsem.at[i])
         for i, (src, dst) in enumerate(
-            ((w_hbm, w), (e_hbm, e), (ep_hbm, ep), (cen_hbm, cen), (off_hbm, off))
+            ((h_hbm, hbuf.at[zh, x, core]), (w_hbm, w), (e_hbm, e), (ep_hbm, ep), (cen_hbm, cen), (off_hbm, off))
         )
     ]
     for copy in loads:
         copy.start()
-
-    barrier = pltpu.get_barrier_semaphore()
-    peers = [core_dev, zl_dev, *x_dev.values(), *z_dev.values(), *y_dev.values()]
-    for dev in peers:
-        pl.semaphore_signal(barrier, inc=1, device_id=dev, device_id_type=MESH)
-    hbuf[zh, x, core] = jnp.transpose(h_ref[...].astype(F32)).astype(BF)
     pl.semaphore_wait(barrier, len(peers))
 
     def block(buf, q, i, c):
         return buf.at[(zh + q) % NZ, (x + i) % NX, c]
 
-    def spread(buf, name, q):
+    def spread(buf, name, q, src=None):
         mine = block(buf, q, 0, core)
+        src = mine if src is None else src
         for i in far:
-            send(mine, mine, (name, "x", (NX - i) % NX, q), x_dev[i])
-        send(mine, mine, (name, "c", 0, q), core_dev)
-
-    def gather_start(buf, name):
+            send(src, mine, (name, "x", (NX - i) % NX, q), x_dev[i])
+        send(src, mine, (name, "c", 0, q), core_dev)
+
+    def gather_start(buf, name, src=None):
         mine = block(buf, 0, 0, core)
+        src = mine if src is None else src
         for q in far:
-            send(mine, mine, (name, "z", (NZ - q) % NZ), z_dev[q])
-        spread(buf, name, 0)
+            send(src, mine, (name, "z", (NZ - q) % NZ), z_dev[q])
+        spread(buf, name, 0, src)
 
     def from_z(buf, name, q):
         arrive(block(buf, q, 0, core), (name, "z", q))
@@ -120,22 +120,19 @@
         for i in range(NX):
             arrive(block(buf, q, i, mate), (name, "c", i, q))
 
-    gather_start(hbuf, "h")
-    loads[0].wait()
-    loads[1].wait()
-    for i in range(32):
-        wt[:, i * B:(i + 1) * B] = jnp.transpose(w[i * B:(i + 1) * B, :].astype(F32)).astype(BF)
+    gather_start(hbuf, "h", h_hbm)
+    for copy in loads:
+        copy.wait()
     for i in range(4):
         et[i * B:(i + 1) * B, :] = jnp.transpose(e[:, i * B:(i + 1) * B].astype(F32)).astype(BF)
-    for copy in loads[2:]:
-        copy.wait()
-
     def to_planes(q):
         zq = (zh + q) % NZ
         near_by = (zq + NY - y) % NZ
+        for i in range(NX):
+            ht[zq, i] = jnp.transpose(hbuf[zq, i, core].astype(F32)).astype(BF)
         for k, ahead in enumerate((near_by + NZ, near_by)):
             copy = pltpu.make_async_remote_copy(
-                hbuf.at[zq, :, core],
+                ht.at[zq],
                 fy.at[y, :, core],
                 fsend.at[q, k],
                 frecv.at[(NY - ahead) % NY],
@@ -164,7 +161,8 @@
     for q in (0, 1, 3, 2):
         from_core(hbuf, "h", q)
 
-    pbuf[zh, x, core] = dot(wt[...], hbuf[...].reshape(32 * B, B)).astype(BF)
+    feats = [hbuf[i // 8, (i // 2) % NX, i % 2] for i in range(8 * NZ)]
+    pbuf[zh, x, core] = jnp.transpose(dot(jnp.concatenate(feats, 1), w[...])).astype(BF)
     gather_start(pbuf, "p")
     def core_step(p, r, name, q):
         send(p.at[q, mate], r.at[q], (name, "c", q), core_dev)
@@ -200,9 +198,9 @@
 
     def grads(q):
         zq = (zh + q) % NZ
-        for h in range(2):
+        def one_piece(h, carry):
             p = zq * 2 + h
-            proj = pbuf[zq, 2 * h:2 * h + 2].reshape(4 * B, B)
+            proj = pbuf[zq, pl.ds(2 * h, 2)].reshape(4 * B, B)
             logits = dot(e[...], proj)
             inside = piece == p
             exposure = jnp.where(piece > p, 1.0, jnp.where(inside, offset, 0.0))
@@ -212,6 +210,9 @@
             out = dot(et[...], grad).astype(BF)
             for j in range(4):
                 part[q, j % 2, 2 * h + j // 2] = out[j * B:(j + 1) * B]
+            return carry
+
+        lax.fori_loop(0, 2, one_piece, 0)
         core_step(part, crecv, "g", q)
 
     def reduce_x(q):
@@ -284,7 +285,9 @@
             got, got, fsend.at[0, 0], frecv.at[i], device_id=core_dev, device_id_type=MESH
         ).wait_recv()
         send(got, got, ("fc", i), core_dev)
-    fy[y] = hbuf[chunk]
+    for i in range(NX):
+        fy[y, i, core] = ht[chunk, i]
+        fy[y, i, mate] = jnp.transpose(hbuf[chunk, i, mate].astype(F32)).astype(BF)
     pgy[y] = pg[...]
 
     arrive(epeer, ("ez",))
@@ -390,7 +393,6 @@
     scale = 1.0 / math.sqrt(rows * lax.axis_size("dp"))
     tasks, rank = task_embed.shape
     features, cols = proj_weight.shape
-    vmem = pl.BlockSpec(memory_space=pltpu.VMEM)
     hbm = pl.BlockSpec(memory_space=pl.ANY)
 
     def reduce_buffers():
@@ -410,7 +412,7 @@
             jax.ShapeDtypeStruct((NZ, NX, 2, B, cols), BF),
             jax.ShapeDtypeStruct((NY, tasks // NY, rank), BF),
         ),
-        in_specs=[vmem] + [hbm] * 5,
+        in_specs=[hbm] * 6,
         out_specs=(hbm, hbm, hbm),
         scratch_shapes=[
             pltpu.VMEM((features, cols), BF),
@@ -418,12 +420,12 @@
             pltpu.VMEM((tasks, rows), jnp.int32),
             pltpu.VMEM((tasks, rows), jnp.int32),
             pltpu.VMEM((tasks, rows), jnp.int32),
-            pltpu.VMEM((cols, features), BF),
             pltpu.VMEM((rank, tasks), BF),
             pltpu.VMEM((NZ, NX, 2, B, B), BF),
             pltpu.VMEM((NZ, NX, 2, B, B), BF),
             pltpu.VMEM((8, tasks, rows), BF),
             pltpu.VMEM((NY, NX, 2, B, B), BF),
+            pltpu.VMEM((NZ, NX, B, B), BF),
             *reduce_buffers(),
             *reduce_buffers(),
             pltpu.VMEM((B, B), BF),
@@ -437,7 +439,7 @@
             pltpu.VMEM((B, rows), BF),
             pltpu.VMEM((NZ, NX, 2, B, cols), BF),
             pltpu.VMEM((NY, tasks // NY, rank), BF),
-            pltpu.SemaphoreType.DMA((5,)),
+            pltpu.SemaphoreType.DMA((6,)),
             pltpu.SemaphoreType.DMA((32,)),
             pltpu.SemaphoreType.DMA((NZ, 2)),
             pltpu.SemaphoreType.DMA((NY,)),

time: 81.8 us -> 80.8 us (0.988)
  Pallas kernels: 80.9 us -> 79.7 us
    pallas_call x1, Pallas kernels: 78.8 us -> 77.6 us  [shards(): pl.pallas_call(functools.partial(kernel, scale), out_shape=(jax.ShapeDtyp...]
where the time goes in v4:
time: 80.8 us; the launch traced here: 80.4 us
  Pallas kernels  79.7 us (99%)
    pallas_call x1, Pallas kernels, shards(): pl.pallas_call(functools.partial(kernel, scale), out_shape=(jax.ShapeDtyp...  77.6 us
    pallas_call x1, Pallas kernels, move_results(): pl.pallas_call(move_kernel, out_shape=[jax.ShapeDtypeStruct(r.shape, r.dt...  2.1 us

profile of v4, /device:TPU:1, one launch (start us, length us, event | category | flops | bytes accessed | tf_op | source)
XLA Modules:
  0.0 80.4 jit_solution(4688254802756274432)
XLA Ops:
  0.6 77.6 %shard_map.85 = (bf16[128,128]{1,0:T(8,128)(2,1)}, bf16[4,4,2,128,128]{4,3,2,1,0:T(8,128)(2,1)}, bf16[8,32,512]{2,1,0:T(8,128)(2,1)}) custom-call(bf16[128,128]{1,0:T(8,128)(2,1)} %h_hbm.1, bf16[4096,128]{1,0:T(8,128)(2,1)} %w_hbm.1, bf16[256,512]{1,0:T(8,128)(2,1)} %e_hbm.1, s32[256,128]{1,0:T(8,128)} %ep_hbm.1, s32[256,128]{1,0:T(8,128)} %cen_hbm.1, ...), custom_call_target="tpu_custom_call" | custom-call | tf_op jit(solution)/shard_map/pallas_call | solution.py:408
  78.3 2.1 %shard_map.86 = (bf16[128,128]{1,0:T(8,128)(2,1)}, bf16[4,4,2,128,128]{4,3,2,1,0:T(8,128)(2,1)}, bf16[8,32,512]{2,1,0:T(8,128)(2,1)}) custom-call(bf16[128,128]{1,0:T(8,128)(2,1)} %get-tuple-element.9.hg, bf16[4,4,2,128,128]{4,3,2,1,0:T(8,128)(2,1)} %get-tuple-element.10.wg, bf16[8,32,512]{2,1,0:T(8,128)(2,1)} %get-tuple-element.11.eg), custom_call_target="tpu_custom_call" | custom-call | tf_op jit(solution)/shard_map/pallas_call | solution.py:377

commit v5 on v4

--- a/solution.py
+++ b/solution.py
@@ -271,13 +271,6 @@
     x_step(hpart, hcrecv, hs1, hxrecv, "d", 3)
     x_step(hpart, hcrecv, hs1, hxrecv, "d", 0)
 
-    total = epart[y].astype(F32)
-    for i in far_y:
-        arrive(erecv.at[i], ("e", i))
-        total += erecv[i].astype(F32)
-    eown[...] = total.astype(BF)
-    send(eown, epeer, ("ez",), zl_dev)
-
     chunk = y % NZ
     for i in far_y:
         got = fy.at[(y + i) % NY, :, core]
@@ -285,6 +278,14 @@
             got, got, fsend.at[0, 0], frecv.at[i], device_id=core_dev, device_id_type=MESH
         ).wait_recv()
         send(got, got, ("fc", i), core_dev)
+
+    total = epart[y].astype(F32)
+    for i in far_y:
+        arrive(erecv.at[i], ("e", i))
+        total += erecv[i].astype(F32)
+    eown[...] = total.astype(BF)
+    send(eown, epeer, ("ez",), zl_dev)
+
     for i in range(NX):
         fy[y, i, core] = ht[chunk, i]
         fy[y, i, mate] = jnp.transpose(hbuf[chunk, i, mate].astype(F32)).astype(BF)

time: 80.8 us -> 80.8 us (level)
  no operation moved by 1% of the time
where the time goes in v5:
time: 80.8 us; the launch traced here: 80.4 us
  Pallas kernels  79.8 us (99%)
    pallas_call x1, Pallas kernels, shards(): pl.pallas_call(functools.partial(kernel, scale), out_shape=(jax.ShapeDtyp...  77.7 us
    pallas_call x1, Pallas kernels, move_results(): pl.pallas_call(move_kernel, out_shape=[jax.ShapeDtypeStruct(r.shape, r.dt...  2.1 us

profile of v5, /device:TPU:1, one launch (start us, length us, event | category | flops | bytes accessed | tf_op | source)
XLA Modules:
  0.0 80.4 jit_solution(3061358765127229563)
XLA Ops:
  0.6 77.7 %shard_map.85 = (bf16[128,128]{1,0:T(8,128)(2,1)}, bf16[4,4,2,128,128]{4,3,2,1,0:T(8,128)(2,1)}, bf16[8,32,512]{2,1,0:T(8,128)(2,1)}) custom-call(bf16[128,128]{1,0:T(8,128)(2,1)} %h_hbm.1, bf16[4096,128]{1,0:T(8,128)(2,1)} %w_hbm.1, bf16[256,512]{1,0:T(8,128)(2,1)} %e_hbm.1, s32[256,128]{1,0:T(8,128)} %ep_hbm.1, s32[256,128]{1,0:T(8,128)} %cen_hbm.1, ...), custom_call_target="tpu_custom_call" | custom-call | tf_op jit(solution)/shard_map/pallas_call | solution.py:409
  78.3 2.1 %shard_map.86 = (bf16[128,128]{1,0:T(8,128)(2,1)}, bf16[4,4,2,128,128]{4,3,2,1,0:T(8,128)(2,1)}, bf16[8,32,512]{2,1,0:T(8,128)(2,1)}) custom-call(bf16[128,128]{1,0:T(8,128)(2,1)} %get-tuple-element.9.hg, bf16[4,4,2,128,128]{4,3,2,1,0:T(8,128)(2,1)} %get-tuple-element.10.wg, bf16[8,32,512]{2,1,0:T(8,128)(2,1)} %get-tuple-element.11.eg), custom_call_target="tpu_custom_call" | custom-call | tf_op jit(solution)/shard_map/pallas_call | solution.py:378
